TPU v7x, 512 devices: a whole 4x8x8 slice. The times are simulated.
512 devices in a mesh: col: 8 (over y_lo, core), dev: 64 (over y_hi, z, x).
Axes of the slice: x: 4, y: 8 (y_hi: 2, y_lo: 4; y = y_hi * 4 + y_lo), z: 8, core: 2. Of those that a mesh axis runs over, the one named last changes fastest.
Arguments:
- factor_a: float32 [1536, 16, 512], P('dev'), may hold values from -1 to 1
- factor_b: float32 [1536, 64, 512], P('dev', 'col'), may hold values from -1 to 1
- factor_occ: float32 [1536, 16, 512], P('dev'), may hold values from -1 to 1
- singles_a: float32 [16, 16], replicated, may hold values from -1.5 to 1.5
- singles_b: float32 [16, 64], P(None, 'col'), may hold values from -1.5 to 1.5
- doubles: bfloat16 [512, 512, 256], P('col', 'dev'), may hold values from -0.023925781 to 0.023925781
- orbital_a: float32 [16], P('col'), may hold values from 0.2 to 3
- orbital_b: float32 [64], P('dev'), may hold values from 0.2 to 3
- orbital_occ: float32 [16], replicated, may hold values from -2 to -0.3
Outputs:
- update: float32 [16, 64, 256], P('col', 'dev')
All inputs are finite; a program needn't handle non-finite values.
Results may differ from a plain program's by a relative error of at most 0.0049.
Values may be sent and summed in bfloat16 or wider, within the bound.
A program may use at most 64 MiB of HBM per device.

v0:
```python
import jax
import jax.numpy as jnp
from jax import lax
from jax.sharding import PartitionSpec as P


def body(
    factor_a, factor_b, factor_occ, singles_a, singles_b, doubles, orbital_a, orbital_b, orbital_occ
):
    highest = lax.Precision.HIGHEST
    c_tile = doubles.shape[0]
    d_tile = doubles.shape[1]
    pair_count = doubles.shape[2]
    shard_rows = factor_a.shape[0]
    a_rows = factor_a.shape[1]
    d_groups = factor_b.shape[2] // d_tile
    col_index = lax.axis_index("col")
    occ_tile = lax.dynamic_slice_in_dim(factor_occ, col_index * c_tile, c_tile, 2)
    a_tile = lax.dynamic_slice_in_dim(factor_a, col_index * c_tile, c_tile, 2)
    dressed_a = (a_tile - jnp.einsum("ka,qkc->qac", singles_a, occ_tile, precision=highest)).astype(
        jnp.bfloat16
    )
    dressed_a = dressed_a.reshape(shard_rows, a_rows * c_tile)
    dressed_b = (
        factor_b - jnp.einsum("kb,qkd->qbd", singles_b, factor_occ, precision=highest)
    ).astype(jnp.bfloat16)
    rows_all = lax.all_gather(dressed_b, "col", axis=1, tiled=True)
    b_rows_all = rows_all.shape[1]
    grouped = rows_all.reshape(shard_rows, b_rows_all, d_groups, d_tile)
    grouped = jnp.transpose(grouped, (0, 2, 1, 3)).reshape(
        shard_rows, d_groups, b_rows_all * d_tile
    )
    moved = lax.all_to_all(grouped, "dev", split_axis=1, concat_axis=0, tiled=True)
    whole_b = moved.reshape(moved.shape[0], -1)
    b_rows_all = whole_b.shape[1] // d_tile
    contract_first = (((0,), (0,)), ((), ()))
    whole_a = lax.all_gather(dressed_a, "dev", axis=0, tiled=True)
    integral = lax.dot_general(whole_a, whole_b, contract_first, preferred_element_type=jnp.float32)
    integral = integral.astype(jnp.bfloat16).reshape(a_rows, c_tile, b_rows_all, d_tile)
    integral = jnp.transpose(integral, (0, 2, 1, 3)).reshape(a_rows * b_rows_all, c_tile * d_tile)
    partial_value = jnp.dot(
        integral, doubles.reshape(c_tile * d_tile, pair_count), preferred_element_type=jnp.float32
    )
    partial_value = partial_value.reshape(a_rows, b_rows_all, pair_count)
    reduced = lax.psum_scatter(partial_value, "dev", scatter_dimension=1, tiled=True)
    total = lax.psum_scatter(reduced, "col", scatter_dimension=0, tiled=True)
    pair_energy = (orbital_occ[:, None] + orbital_occ[None, :]).reshape(-1)
    denominator = orbital_a[:, None, None] + orbital_b[None, :, None] - pair_energy[None, None, :]
    return total / denominator


def solution(mesh):
    return jax.shard_map(
        body,
        mesh=mesh,
        in_specs=(
            P("dev", None, None),
            P("dev", "col", None),
            P("dev", None, None),
            P(),
            P(None, "col"),
            P("col", "dev", None),
            P("col"),
            P("dev"),
            P(),
        ),
        out_specs=P("col", "dev", None),
        check_vma=False,
    )
```

profile of v0, /device:TPU:1, one launch (start us, length us, event | category | flops | bytes accessed | tf_op | source)
XLA Modules:
  0.0 714.7 jit_solution(8249692002151963328)
XLA Ops:
  6.5 0.0 copy-start
  6.5 0.0 all-gather.5.cloned.1.call-start
  6.5 1.1 copy-done
  7.7 2.2 fusion.1
  9.9 0.0 all-gather.5.cloned.1.call-update
  9.9 0.0 all-gather.3.cloned.1.call-start
  10.0 1.4 fusion.3
  11.3 0.7 reshape.86
  12.1 0.0 all-gather.3.cloned.1.call-update
  12.1 0.0 reduce-scatter.2.cloned.1.call-start
  12.1 42.0 %all-gather.5.cloned.1.call-done = bf16[24,64,512]{2,1,0:T(8,128)(2,1)} async-done(((bf16[24,8,512]{2,1,0:T(8,128)(2,1)}), bf16[24,64,512]{2,1,0:T(8,128)(2,1)}) %all-gather.5.cloned.1.call-update) | async-done | bytes 1572880 | tf_op jit(solution)/shard_map/all_gather | solution.py:27
  54.2 4.1 copy.21
  58.3 5.4 copy.22
  63.7 3.9 copy.23
  67.6 53.7 %all_to_all.15 = bf16[24,64,512]{2,0,1:T(8,128)(2,1)} all-to-all(bf16[24,64,512]{2,0,1:T(8,128)(2,1)S(1)} %copy.23), channel_id=1, replica_groups=mesh['col'=8,'dev'=64] {'dev'}, dimensions={1} | all-to-all | bytes 3145728 | tf_op jit(solution)/shard_map/all_to_all | solution.py:33
  121.3 96.4 %all-gather.3.cloned.1.call-done = bf16[1536,1024]{1,0:T(8,128)(2,1)} async-done(((bf16[24,1024]{1,0:T(8,128)(2,1)}), bf16[1536,1024]{1,0:T(8,128)(2,1)}) %all-gather.3.cloned.1.call-update) | async-done | bytes 3145744 | tf_op jit(solution)/shard_map/all_gather | solution.py:37
  217.7 4.2 convolution_convert_fusion
  221.9 1.3 copy.24
  223.2 2.9 reshape.90
  226.2 0.0 copy-start.1
  226.2 6.6 copy.29
  232.7 0.0 copy-done.1
  232.7 0.0 copy-start.2
  232.7 0.0 copy-start.3
  232.7 6.8 convolution_bitcast_fusion
  239.6 0.0 reduce-scatter.2.cloned.1.call-update
  239.6 0.0 copy-done.2
  239.6 0.1 broadcast_add_fusion
  239.7 0.1 add.46
  240.4 1.3 dynamic-slice
  242.3 0.0 copy-done.3
  242.4 389.7 %reduce-scatter.2.cloned.1.call-done = f32[16,1,256]{2,0,1:T(8,128)} async-done(((f32[16,64,256]{2,0,1:T(8,128)}), f32[16,1,256]{2,0,1:T(8,128)}) %reduce-scatter.2.cloned.1.call-update) | async-done | bytes 16400 | tf_op jit(solution)/shard_map/reduce_scatter | solution.py:45
  632.1 0.7 copy.27
  632.8 74.7 %all-reduce = f32[16,1,256]{2,1,0:T(1,128)S(1)} all-reduce(f32[16,1,256]{2,1,0:T(1,128)S(1)} %copy.27), channel_id=3, replica_groups=mesh['col'=8,'dev'=64] {'col'}, use_global_device_ids=true, to_apply=%region_1.0.clone | all-reduce | flops 4096 | bytes 32768
  707.5 0.7 dynamic-slice_divide_fusion
  (1 shorter events, 0.0 us)
Async XLA Ops:
  6.5 1.1 copy-start
  6.5 47.6 %all-gather.5.cloned.1.call-start = ((), (), s32[]{:S(2)}) async-start(), calls=%async_computation.3 | async-start | bytes 1769472 | tf_op jit(solution)/shard_map/all_gather | solution.py:27
  9.9 207.8 %all-gather.3.cloned.1.call-start = ((), (), s32[]{:S(2)}) async-start(), calls=%async_computation.2 | async-start | bytes 3194880 | tf_op jit(solution)/shard_map/all_gather | solution.py:37
  12.1 620.0 %reduce-scatter.2.cloned.1.call-start = ((), (), s32[]{:S(2)}) async-start(), calls=%async_computation.4 | async-start | bytes 1064960 | tf_op jit(solution)/shard_map/reduce_scatter | solution.py:45
  226.2 6.6 copy-start.1
  232.7 6.8 copy-start.2
  232.7 9.6 %copy-start.3 = (f32[2]{0:T(128)S(1)}, f32[2]{0:T(128)}, u32[]{:S(2)}) copy-start(f32[2]{0:T(128)} %param.15) | copy-start | bytes 28
Sparse Core Ops, SparseCore 0:
  10.0 44.0 all-gather.4
  58.7 158.9 all-gather.2
  239.7 392.3 reduce-scatter.1
where the time goes:
time: 715 us
  waiting for transfers between devices  528 us (74%)
  blocking collectives  128 us (18%)
  local copies, waits for them, and re-layouts  28.2 us (4%)
  matrix products  14.5 us (2%)
  between operations  14.5 us (2%)
    reduce_scatter x1, waiting for transfers between devices, body(): lax.psum_scatter(partial_value, 'dev', scatter_dimension=1, tiled=True)  390 us
    all_gather x1, waiting for transfers between devices, body(): whole_a = lax.all_gather(dressed_a, 'dev', axis=0, tiled=True)  96.4 us
    unnamed x1, blocking collectives  74.7 us
    all_to_all x1, blocking collectives, body(): lax.all_to_all(grouped, 'dev', split_axis=1, concat_axis=0, tiled=True)  53.7 us
    all_gather x1, waiting for transfers between devices, body(): rows_all = lax.all_gather(dressed_b, 'col', axis=1, tiled=True)  42 us
  transfers between devices with their start and end apart: 3, of which 3 were waited for; matrix products, arithmetic and copies ran while one was open for 2% of the time, Pallas kernels for 0%

commit v1 on v0

--- a/solution.py
+++ b/solution.py
@@ -30,7 +30,10 @@
     grouped = jnp.transpose(grouped, (0, 2, 1, 3)).reshape(
         shard_rows, d_groups, b_rows_all * d_tile
     )
-    moved = lax.all_to_all(grouped, "dev", split_axis=1, concat_axis=0, tiled=True)
+    moved = jnp.concatenate(
+        lax.all_to_all(jnp.stack(jnp.split(grouped, lax.axis_size("dev"), axis=1)), "dev", 0, 0),
+        axis=0,
+    )
     whole_b = moved.reshape(moved.shape[0], -1)
     b_rows_all = whole_b.shape[1] // d_tile
     contract_first = (((0,), (0,)), ((), ()))

time: 715 us -> 809 us (1.13)
  local copies, waits for them, and re-layouts: 28.2 us -> 213 us
  waiting for transfers between devices: 528 us -> 430 us
    split x0 -> x4, local copies, waits for them, and re-layouts: none -> 189 us  [body(): jnp.split(grouped, lax.axis_size('dev'), axis=1)]
    all_gather x1, waiting for transfers between devices: 96.4 us -> 0.01 us  [body(): whole_a = lax.all_gather(dressed_a, 'dev', axis=0, tiled=True)]
  transfers between devices with their start and end apart: 3 -> 3, of which waited for: 3 -> 2; matrix products, arithmetic and copies ran while one was open for 2% -> 25% of each run, Pallas kernels for 0% -> 0%
where the time goes in v1:
time: 809 us; the launch traced here: 802 us
  waiting for transfers between devices  430 us (53%)
  local copies, waits for them, and re-layouts  213 us (26%)
  blocking collectives  129 us (16%)
  between operations  15.3 us (2%)
  matrix products  14.1 us (2%)
    reduce_scatter x1, waiting for transfers between devices, body(): lax.psum_scatter(partial_value, 'dev', scatter_dimension=1, tiled=True)  387 us
    split x4, local copies, waits for them, and re-layouts, body(): jnp.split(grouped, lax.axis_size('dev'), axis=1)  189 us
    unnamed x1, blocking collectives  75.2 us
    all_to_all x1, blocking collectives, body(): lax.all_to_all(jnp.stack(jnp.split(grouped, lax.axis_size('dev'), axis=1)...  54 us
    all_gather x1, waiting for transfers between devices, body(): rows_all = lax.all_gather(dressed_b, 'col', axis=1, tiled=True)  42 us
  transfers between devices with their start and end apart: 3, of which 2 were waited for; matrix products, arithmetic and copies ran while one was open for 25% of the time, Pallas kernels for 0%

profile of v1, /device:TPU:1, one launch (start us, length us, event | category | flops | bytes accessed | tf_op | source)
XLA Modules:
  0.0 802.3 jit_solution(4617937562389698255)
XLA Ops:
  6.5 0.0 copy-start
  6.5 0.0 copy-start.2
  6.5 0.0 all-gather.5.cloned.1.call-start
  6.5 1.1 copy-done
  7.7 2.2 fusion.1
  9.9 0.0 all-gather.5.cloned.1.call-update
  9.9 0.0 all-gather.3.cloned.1.call-start
  10.0 0.0 copy-done.2
  10.0 1.3 fusion.3
  11.3 0.7 reshape.82
  12.1 0.0 all-gather.3.cloned.1.call-update
  12.1 0.0 reduce-scatter.2.cloned.1.call-start
  12.1 42.0 %all-gather.5.cloned.1.call-done = bf16[24,64,512]{2,1,0:T(8,128)(2,1)} async-done(((bf16[24,8,512]{2,1,0:T(8,128)(2,1)}), bf16[24,64,512]{2,1,0:T(8,128)(2,1)}) %all-gather.5.cloned.1.call-update) | async-done | bytes 1572880 | tf_op jit(solution)/shard_map/all_gather | solution.py:27
  54.2 4.1 copy.1658
  58.3 5.4 copy.1659
  63.7 21.9 %slice_reduce_fusion.57 = (bf16[24,512]{1,0:T(8,128)(2,1)S(1)}, bf16[24,512]{1,0:T(8,128)(2,1)S(1)}, bf16[24,512]{1,0:T(8,128)(2,1)S(1)}, bf16[24,512]{1,0:T(8,1...) fusion(bf16[24,64,512]{1,2,0:T(8,128)(2,1)} %bitcast.166), kind=kLoop, calls=%fused_computation.57 | loop fusion | bytes 344064 | tf_op jit(solution)/shard_map/split | solution.py:34
  85.6 55.8 %slice_reduce_fusion.38 = (bf16[24,512]{1,0:T(8,128)(2,1)S(1)}, bf16[24,512]{1,0:T(8,128)(2,1)S(1)}, bf16[24,512]{1,0:T(8,128)(2,1)S(1)}, bf16[24,512]{1,0:T(8,1...) fusion(bf16[24,64,512]{1,2,0:T(8,128)(2,1)} %bitcast.167), kind=kLoop, calls=%fused_computation.38 | loop fusion | bytes 933888 | tf_op jit(solution)/shard_map/split | solution.py:34
  141.5 55.5 %slice_reduce_fusion.19 = (bf16[24,512]{1,0:T(8,128)(2,1)S(1)}, bf16[24,512]{1,0:T(8,128)(2,1)S(1)}, bf16[24,512]{1,0:T(8,128)(2,1)S(1)}, bf16[24,512]{1,0:T(8,1...) fusion(bf16[24,64,512]{1,2,0:T(8,128)(2,1)} %bitcast.168), kind=kLoop, calls=%fused_computation.19 | loop fusion | bytes 933888 | tf_op jit(solution)/shard_map/split | solution.py:34
  197.0 55.5 %slice_reduce_fusion = (bf16[24,512]{1,0:T(8,128)(2,1)S(1)}, bf16[24,512]{1,0:T(8,128)(2,1)S(1)}, bf16[24,512]{1,0:T(8,128)(2,1)S(1)}, bf16[24,512]{1,0:T(8,128)...) fusion(bf16[24,64,512]{1,2,0:T(8,128)(2,1)} %bitcast.169), kind=kLoop, calls=%fused_computation | loop fusion | bytes 933888 | tf_op jit(solution)/shard_map/split | solution.py:34
  253.3 54.0 %all_to_all.5 = bf16[64,24,1,512]{3,1,2,0:T(8,128)(2,1)S(1)} all-to-all(bf16[64,24,1,512]{3,1,2,0:T(8,128)(2,1)S(1)} %constant_dynamic-update-slice_fusion), channel_id=1, replica_groups=mesh['col'=8,'dev'=64] {'dev'}, dimensions={0} | all-to-all | bytes 3145728 | tf_op jit(solution)/shard_map/all_to_all | solution.py:34
  307.2 0.0 all-gather.3.cloned.1.call-done
  307.2 3.7 convolution_convert_fusion
  310.9 1.3 copy.1660
  312.3 2.9 reshape.85
  315.2 0.0 copy-start.1
  315.2 6.5 copy.1665
  321.8 0.0 copy-done.1
  321.8 0.0 copy-start.3
  321.8 0.0 copy-start.4
  321.8 6.8 convolution_bitcast_fusion
  328.6 0.0 reduce-scatter.2.cloned.1.call-update
  328.6 0.0 copy-done.3
  328.7 0.1 broadcast_add_fusion
  328.7 0.1 add.46
  329.5 1.3 dynamic-slice
  331.4 0.0 copy-done.4
  331.4 387.4 %reduce-scatter.2.cloned.1.call-done = f32[16,1,256]{2,0,1:T(8,128)} async-done(((f32[16,64,256]{2,0,1:T(8,128)}), f32[16,1,256]{2,0,1:T(8,128)}) %reduce-scatter.2.cloned.1.call-update) | async-done | bytes 16400 | tf_op jit(solution)/shard_map/reduce_scatter | solution.py:48
  718.9 0.7 copy.1663
  719.6 75.2 %all-reduce = f32[16,1,256]{2,1,0:T(1,128)S(1)} all-reduce(f32[16,1,256]{2,1,0:T(1,128)S(1)} %copy.1663), channel_id=3, replica_groups=mesh['col'=8,'dev'=64] {'col'}, use_global_device_ids=true, to_apply=%region_1.0.clone | all-reduce | flops 4096 | bytes 32768
  794.8 0.7 dynamic-slice_divide_fusion
  (65 shorter events, 0.3 us)
Async XLA Ops:
  6.5 1.1 copy-start
  6.5 3.4 copy-start.2
  6.5 47.6 %all-gather.5.cloned.1.call-start = ((), (), s32[]{:S(2)}) async-start(), calls=%async_computation.3 | async-start | bytes 1769472 | tf_op jit(solution)/shard_map/all_gather | solution.py:27
  9.9 297.3 %all-gather.3.cloned.1.call-start = ((), (), s32[]{:S(2)}) async-start(), calls=%async_computation.2 | async-start | bytes 3194880 | tf_op jit(solution)/shard_map/all_gather | solution.py:40
  12.1 706.8 %reduce-scatter.2.cloned.1.call-start = ((), (), s32[]{:S(2)}) async-start(), calls=%async_computation.4 | async-start | bytes 1064960 | tf_op jit(solution)/shard_map/reduce_scatter | solution.py:48
  315.2 6.6 copy-start.1
  321.8 6.9 copy-start.3
  321.8 9.6 %copy-start.4 = (f32[2]{0:T(128)S(1)}, f32[2]{0:T(128)}, u32[]{:S(2)}) copy-start(f32[2]{0:T(128)} %param.15) | copy-start | bytes 28
Sparse Core Ops, SparseCore 0:
  10.0 44.0 all-gather.4
  58.7 140.5 all-gather.2
  328.8 390.0 reduce-scatter.1
